TPU v7x, 512 devices: a whole 4x4x16 slice. The times are simulated.
512 devices in a mesh: blk: 128 (over y, x_lo, z), quad: 4 (over x_hi, core).
Axes of the slice: x: 4 (x_hi: 2, x_lo: 2; x = x_hi * 2 + x_lo), y: 4, z: 16, core: 2. Of those that a mesh axis runs over, the one named last changes fastest.
Arguments:
- positions: float32 [3, 16384], P(None, ('blk', 'quad')), may hold values from 0 to 1
- forces: float32 [3, 16, 16384], P(None, None, ('blk', 'quad')), may hold values from -6 to 6
Outputs:
- velocity: float32 [3, 16, 16384], P(None, None, ('blk', 'quad'))
All inputs are finite; a program needn't handle non-finite values.
Results may differ from a plain program's by a relative error of at most 0.0003.
Values sent between devices are 32-bit elements; how exact they have to be, the bound alone decides.
A program may use at most 64 MiB of HBM per device.

v0:
```python
import math

import jax
import jax.numpy as jnp
from jax import lax
from jax.sharding import PartitionSpec as P

radius_scale = 0.3


def laid_out(tiles, dim):
    lengths = list(tiles.shape[1:])
    lengths[dim] *= tiles.shape[0]
    return jnp.moveaxis(tiles, 0, dim).reshape(lengths)


def copy_for_each(value, axis):
    peers = lax.axis_size(axis)
    return lax.all_to_all(
        jnp.broadcast_to(value[None], (peers, *value.shape)), axis, 0, 0, tiled=True
    )


def gather_directly(value, axis, dim):
    return laid_out(copy_for_each(value, axis), dim)


def gather_turned(arrays, axis, dims):
    turned = [jnp.moveaxis(a, dim, 0) for a, dim in zip(arrays, dims)]
    widths = [t[0].size for t in turned]
    both = jnp.concatenate([t.reshape(-1, w) for t, w in zip(turned, widths)], axis=1)
    whole = lax.all_gather(both, axis, axis=0, tiled=True)
    tiles = jnp.split(whole, [sum(widths[:k]) for k in range(1, len(widths))], axis=1)
    return tuple(
        (
            jnp.moveaxis(b.reshape(-1, *t.shape[1:]), 0, dim)
            for b, t, dim in zip(tiles, turned, dims)
        )
    )


def in_blocks(value, dim, peers):
    before, after = (value.shape[:dim], value.shape[dim + 1 :])
    return jnp.moveaxis(value.reshape(*before, peers, -1, *after), dim, 0)


def sent_and_summed(value, axis, dim):
    peers = lax.axis_size(axis)
    tiles = lax.all_to_all(in_blocks(value, dim, peers), axis, 0, 0, tiled=True)
    return jnp.sum(tiles, axis=0)


def mobility_tile(home_pos, visit_pos, radius):
    separation = home_pos[:, :, None] - visit_pos[:, None, :]
    squared = jnp.sum(separation * separation, axis=0)
    distance = jnp.sqrt(squared)
    far_dist = jnp.maximum(distance, 2.0 * radius)
    inverse = 1.0 / far_dist
    ratio_sq = radius * radius * inverse * inverse
    factor = 0.75 * radius * inverse
    iso_far = factor * (1.0 + 2.0 / 3.0 * ratio_sq)
    dyad_far = factor * (1.0 - 2.0 * ratio_sq) * inverse * inverse
    iso_near = 1.0 - 9.0 / 32.0 * distance / radius
    dyad_near = 3.0 / 32.0 / (radius * jnp.maximum(distance, radius / 1000.0))
    near_mask = distance < 2.0 * radius
    coef_iso = jnp.where(near_mask, iso_near, iso_far)
    coef_dyad = jnp.where(near_mask, dyad_near, dyad_far)
    identity = jnp.eye(3, dtype=jnp.float32)
    return (
        coef_dyad[None, None] * separation[:, None] * separation[None, :]
        + identity[:, :, None, None] * coef_iso[None, None]
    )


def body(positions, forces):
    vectors = forces.shape[1]
    local_rows = positions.shape[1]
    total = local_rows * lax.axis_size("blk") * lax.axis_size("quad")
    radius = radius_scale / total ** (1.0 / 3.0)
    flat_force = forces.reshape(3 * vectors, local_rows)
    block_pos = gather_directly(positions, "quad", 1)
    block_rows = block_pos.shape[1]
    partial_sum = jnp.zeros((3, vectors, block_rows), jnp.float32)
    part_pos, part_force = gather_turned((positions, flat_force), "blk", (1, 1))
    count = part_pos.shape[1]
    width = math.gcd(count, 512)

    def one_block(index, running):
        col_pos = lax.dynamic_slice_in_dim(part_pos, index * width, width, 1)
        col_force = lax.dynamic_slice_in_dim(part_force, index * width, width, 1).reshape(
            3, vectors, width
        )
        kernel = mobility_tile(block_pos, col_pos, radius)
        return running + jnp.einsum(
            "cdij,dvj->cvi", kernel, col_force, precision=lax.Precision.HIGHEST
        )

    partial_sum = lax.fori_loop(0, count // width, one_block, partial_sum)
    velocity = sent_and_summed(partial_sum, "quad", 2)
    return velocity


def solution(mesh):
    in_specs = (P(None, ("blk", "quad")), P(None, None, ("blk", "quad")))
    out_specs = P(None, None, ("blk", "quad"))
    return jax.shard_map(body, mesh=mesh, in_specs=in_specs, out_specs=out_specs, check_vma=False)
```

profile of v0, /device:TPU:1, one launch (start us, length us, event | category | flops | bytes accessed | tf_op | source)
XLA Modules:
  0.0 370.5 jit_solution(10042499356964226688)
XLA Ops:
  0.0 1.3 broadcast_in_dim.28
  1.3 10.1 %all-to-all-start = ((f32[4,3,32]{2,1,0:T(4,128)}), f32[4,3,32]{2,1,0:T(4,128)S(1)}, u32[]{:S(2)}, u32[]{:S(2)}) async-start(f32[4,3,32]{2,1,0:T(4,128)} %broadcast_in_dim.28), calls=%async_computation | async-start | bytes 16384 | tf_op jit(solution)/shard_map/all_to_all | solution.py:19
  11.4 0.7 pad_maximum_fusion
  12.2 262.2 %all_gather.3 = f32[4096,51]{1,0:T(8,128)S(1)} all-gather(f32[32,51]{1,0:T(8,128)S(1)} %copy.8), channel_id=1, replica_groups=mesh['blk'=128,'quad'=4] {'blk'}, dimensions={0}, use_global_device_ids=true | all-gather | bytes 842112 | tf_op jit(solution)/shard_map/all_gather | solution.py:32
  274.4 1.5 slice_bitcast_fusion
  275.9 0.6 slice_bitcast_fusion.1
  276.5 2.2 copy.11
  278.7 0.6 copy.9
  279.5 0.5 copy-done
  280.0 22.7 %while.17 = (s32[]{:T(128)}, f32[3,16,128]{2,1,0:T(8,128)S(1)}, f32[48,4096]{1,0:T(8,128)S(1)}, f32[3,4,32]{2,1,0:T(4,128)}, f32[3,4096]{1,0:T(4,128)S(1)}, /*in...) while((s32[]{:T(128)}, f32[3,16,128]{2,1,0:T(8,128)S(1)}, ...), condition=%wide.wide.region_2.3_spmd.clone, body=%wide.wide.region_0.2_spmd.clone.sunk | while | flops 117321752 | bytes 5090549 | solution.py:98
  280.0 0.1 multiply_reduce_fusion.3
  280.1 0.3 fusion.29
  280.4 0.2 subtract_multiply_fusion.3
  280.6 2.2 fusion.31
  282.8 0.1 multiply_reduce_fusion.3
  283.0 0.3 fusion.29
  283.2 0.2 subtract_multiply_fusion.3
  283.4 2.2 fusion.31
  285.7 0.1 multiply_reduce_fusion.3
  285.8 0.3 fusion.29
  286.1 0.2 subtract_multiply_fusion.3
  286.3 2.2 fusion.31
  288.5 0.1 multiply_reduce_fusion.3
  288.7 0.3 fusion.29
  288.9 0.2 subtract_multiply_fusion.3
  289.1 2.2 fusion.31
  291.4 0.1 multiply_reduce_fusion.3
  291.5 0.3 fusion.29
  291.8 0.2 subtract_multiply_fusion.3
  291.9 2.2 fusion.31
  294.2 0.1 multiply_reduce_fusion.3
  294.4 0.3 fusion.29
  294.6 0.2 subtract_multiply_fusion.3
  294.8 2.2 fusion.31
  297.1 0.1 multiply_reduce_fusion.3
  297.2 0.3 fusion.29
  297.5 0.2 subtract_multiply_fusion.3
  297.6 2.2 fusion.31
  299.9 0.1 multiply_reduce_fusion.3
  300.0 0.3 fusion.29
  300.3 0.2 subtract_multiply_fusion.3
  300.5 2.2 fusion.31
  302.7 0.1 reshape.69
  302.8 0.1 reshape.73
  302.9 65.6 %all_to_all.10 = f32[4,1,1536]{2,1,0:T(1,128)S(1)} all-to-all(f32[4,1,1536]{2,1,0:T(1,128)S(1)} %reshape.73), channel_id=1, replica_groups=mesh['blk'=128,'quad'=4] {'quad'}, dimensions={0} | all-to-all | bytes 49152 | tf_op jit(solution)/shard_map/all_to_all | solution.py:49
  368.5 0.5 broadcast.294
  369.0 0.7 reduce
  369.8 0.6 reduce_sum.25
  (32 shorter events, 0.5 us)
Async XLA Ops:
  1.3 278.1 %all-to-all-start = ((f32[4,3,32]{2,1,0:T(4,128)}), f32[4,3,32]{2,1,0:T(4,128)S(1)}, u32[]{:S(2)}, u32[]{:S(2)}) async-start(f32[4,3,32]{2,1,0:T(4,128)} %broadcast_in_dim.28), calls=%async_computation | async-start | bytes 16384 | tf_op jit(solution)/shard_map/all_to_all | solution.py:19
  279.4 0.6 copy-start
where the time goes:
time: 371 us; the launch traced here: 370 us
  blocking collectives  328 us (88%)
  matrix products  17.5 us (5%)
  starting transfers between devices  10.1 us (3%)
  local copies, waits for them, and re-layouts  7.87 us (2%)
  other arithmetic  6.63 us (2%)
    all_gather x1, blocking collectives, gather_turned(): whole = lax.all_gather(both, axis, axis=0, tiled=True)  262 us
    all_to_all x1, blocking collectives, sent_and_summed(): tiles = lax.all_to_all(in_blocks(value, dim, peers), axis, 0, 0, tiled=True)  65.6 us
    dot_general x8, matrix products, one_block(): jnp.einsum('cdij,dvj->cvi', kernel, col_force, precision=lax.Precision.HI...  17.5 us
    all_to_all x1, starting transfers between devices, copy_for_each(): lax.all_to_all(jnp.broadcast_to(value[None], (peers, *value.shape)), axis...  10.1 us
  transfers between devices with their start and end apart: 1, of which 0 were waited for; matrix products, arithmetic and copies ran while one was open for 2% of the time, Pallas kernels for 0%

commit v1 on v0

v1 whole, which is shorter than its diff:
```python
import functools

import jax
import jax.numpy as jnp
from jax import lax
from jax.experimental import pallas as pl
from jax.experimental.pallas import tpu as pltpu
from jax.sharding import PartitionSpec as P

MESH = pl.DeviceIdType.MESH
F32 = jnp.float32
BF16 = jnp.bfloat16

radius_scale = 0.3

NX, NY, NZ = 4, 4, 16
PLANE = NX * NY * 2
REACH = NZ // 4
LANES = 128
ROWS = 32
HALF = ROWS // 2
GROUPS = LANES // HALF
FILL = 4


def place():
    blk, quad = lax.axis_index("blk"), lax.axis_index("quad")
    x = (quad // 2) * 2 + (blk // NZ) % 2
    return x, blk // (2 * NZ), blk % NZ, quad % 2


def device(x, y, z, core):
    return ((y * 2 + x % 2) * NZ + z, (x // 2) * 2 + core)


def plane_peers():
    offsets = [(a, b, c) for a in range(NX) for b in range(NY) for c in range(2)]
    far_first = sorted(offsets, key=lambda o: -(min(o[0], NX - o[0]) + min(o[1], NY - o[1])))
    return [o for o in far_first if o != (0, 0, 0)]


def target_offset(step):
    far = step - FILL
    rest = step - (FILL + NZ - 1 - 2 * REACH)
    sign = lambda odd: 1 - 2 * odd
    first = (REACH - step // 2) * sign(step % 2)
    middle = (NZ // 2 - (far + 1) // 2) * sign(1 - far % 2)
    last = (REACH - FILL // 2 - rest // 2) * sign(rest % 2)
    return jnp.where(step < FILL, first, jnp.where(far < NZ - 1 - 2 * REACH, middle, last))


def widened(value):
    return jnp.concatenate([value, jnp.zeros((value.shape[0], LANES - ROWS), F32)], axis=1)


def kernel(radius, pos_hbm, force_hbm, out_ref, pos_in, force_in, my_row, my_block, src_row, src_block, target_row,
           weights, src_pos, sent, landed, in_sem, send_sem, near_sem, far_sem, row_sem, block_sem, part_sem):
    x, y, z, core = place()
    plane_slot = x * GROUPS + y * 2 + core
    turn = (y * 2 + core) * HALF
    load_pos = pltpu.make_async_copy(pos_hbm, pos_in, in_sem.at[0])
    load_force = pltpu.make_async_copy(force_hbm, force_in, in_sem.at[1])
    load_pos.start()
    load_force.start()

    def in_plane(o):
        return device((x + o[0]) % NX, (y + o[1]) % NY, z, (core + o[2]) % 2)

    def on_line(k):
        return device(x, y, (z + k + NZ) % NZ, core)

    line = [k for d in range(REACH, 0, -1) for k in (d, -d)]
    barrier = pltpu.get_barrier_semaphore()
    for k in line:
        pl.semaphore_signal(barrier, 1, device_id=on_line(k), device_id_type=MESH)
    for o in plane_peers():
        pl.semaphore_signal(barrier, 1, device_id=in_plane(o), device_id_type=MESH)

    lane = lax.broadcasted_iota(jnp.int32, (8, LANES), 1)
    sub = lax.broadcasted_iota(jnp.int32, (8, LANES), 0)
    group = lane // HALF

    load_pos.wait()
    mine = [widened(pos_in[e : e + 1, :]) for e in range(3)]
    row = jnp.zeros((1, LANES), F32)
    for h in range(2):
        for e in range(3):
            m = 3 * h + e
            moved = pltpu.roll(mine[e], (HALF * (m - h)) % LANES, 1)
            row = jnp.where(group[0:1] == m, moved, row)
    my_row[0] = pltpu.roll(jnp.broadcast_to(row, (8, LANES)), turn, 1)[0:1]
    load_force.wait()
    parts = [widened(force_in[e]) for e in range(3)]
    dots = sum((mine[e] - 0.5) * parts[e] for e in range(3))
    stack = jnp.concatenate([*parts, dots], axis=0)
    stack = jnp.concatenate([stack, pltpu.roll(stack, LANES - HALF, 1)], axis=0)
    my_block[...] = jnp.transpose(stack)[0:HALF]

    pl.semaphore_wait(barrier, len(line) + len(plane_peers()))

    def send(src, dst, sem, where):
        pltpu.make_async_remote_copy(src, dst, send_sem, sem, device_id=where, device_id_type=MESH).start()

    for k in line:
        sem = near_sem.at[0 if k == -REACH else 1 if k == REACH else 2]
        send(my_row.at[0], target_row.at[z], sem, on_line(k))
    for o in plane_peers():
        send(my_row.at[0], src_row.at[plane_slot], row_sem, in_plane(o))
    for o in plane_peers():
        send(my_block, src_block.at[plane_slot], block_sem, in_plane(o))
    src_row[plane_slot] = my_row[0]
    src_block[plane_slot] = my_block[...]
    target_row[z] = my_row[0]

    def wait(ref, sem):
        pltpu.make_async_copy(ref, ref, sem).wait()

    up, down = (z + REACH) % NZ, (z + NZ - REACH) % NZ
    wait(my_row.at[0], near_sem.at[0])
    for k in range(REACH, 0, -1):
        send(target_row.at[up], target_row.at[up], far_sem, on_line(-k))
    wait(my_row.at[0], near_sem.at[1])
    for k in range(REACH - 1, 0, -1):
        send(target_row.at[down], target_row.at[down], far_sem, on_line(k))

    wait(src_row.at[pl.ds(0, PLANE - 1)], row_sem)
    for tile in range(PLANE // GROUPS):
        rows = jnp.concatenate([src_row[tile * GROUPS + k] for k in range(GROUPS)], axis=0)
        for h in range(2):
            for e in range(3):
                m = 3 * h + e
                own = jnp.sum(jnp.where((group - sub - m + 2 * GROUPS) % GROUPS == 0, rows, 0.0), axis=0, keepdims=True)
                at = (h * PLANE // GROUPS + tile) * LANES
                own = pltpu.roll(jnp.broadcast_to(own, (8, LANES)), (LANES - HALF * m) % LANES, 1)
                src_pos[e, :, at : at + LANES] = own
    wait(target_row.at[pl.ds(0, 2 * REACH - 2)], near_sem.at[2])

    wait(src_block.at[pl.ds(0, PLANE - 1)], block_sem)
    half_rows = PLANE * HALF
    value = src_block[...].reshape(half_rows, LANES)
    high = value.astype(BF16).astype(F32)
    low = value - high
    left = lax.broadcasted_iota(jnp.int32, (half_rows, LANES), 1) < LANES // 2
    weights[0:half_rows] = jnp.where(left, high, pltpu.roll(low, LANES // 2, 1)).astype(BF16)
    weights[half_rows:] = jnp.where(left, pltpu.roll(high, LANES // 2, 1), low).astype(BF16)

    wide = 2 * LANES
    near_sq = 4.0 * radius * radius
    lane_group = lax.broadcasted_iota(jnp.int32, (ROWS, LANES), 1) // HALF

    def one_target(step, carry):
        offset = target_offset(step)
        tz = (z + offset + NZ) % NZ

        @pl.when(step == FILL)
        def _():
            wait(target_row.at[pl.ds(0, NZ - 1 - 2 * REACH)], far_sem)

        theirs = pltpu.roll(jnp.broadcast_to(target_row[tz], (8, LANES)), LANES - turn, 1)
        columns = jnp.transpose(jnp.broadcast_to(theirs[0:1], (LANES, LANES)))
        home = [
            jnp.concatenate([columns[e * HALF : (e + 1) * HALF], columns[(3 + e) * HALF : (4 + e) * HALF]], axis=0)
            for e in range(3)
        ]
        total = jnp.zeros((4 * ROWS, LANES), F32)
        for p in range(2 * half_rows // wide):
            pieces = []
            for q in range(2):
                at = p * wide + q * LANES
                sep = [
                    (home[e].reshape(ROWS // 8, 8, LANES) - src_pos[e, :, at : at + LANES][None]).reshape(ROWS, LANES)
                    for e in range(3)
                ]
                squared = sep[0] * sep[0] + sep[1] * sep[1] + sep[2] * sep[2]
                inverse = lax.rsqrt(jnp.maximum(squared, 1e-30))
                inv_sq = inverse * inverse
                factor = (0.75 * radius) * inverse
                cubed = factor * inv_sq
                near = squared < near_sq
                iso = jnp.where(
                    near, 1.0 - (9.0 / 32.0 / radius) * (squared * inverse), factor + (2.0 / 3.0 * radius * radius) * cubed
                )
                dyad = jnp.where(
                    near,
                    (3.0 / 32.0 / radius) * jnp.minimum(inverse, 1000.0 / radius),
                    cubed * (1.0 - (2.0 * radius * radius) * inv_sq),
                )
                pieces.append(jnp.concatenate([dyad * s for s in sep] + [iso], axis=0))
            exact = jnp.concatenate(pieces, axis=1)
            upper = exact.astype(BF16)
            lower = (exact - upper.astype(F32)).astype(BF16)
            tile = weights[p * wide : (p + 1) * wide, :]
            total += jnp.dot(upper, tile, preferred_element_type=F32)
            total += jnp.dot(lower, tile, preferred_element_type=F32)

        which = lane_group % 4
        scale = jnp.where(which == 0, home[0] - 0.5, jnp.where(which == 1, home[1] - 0.5, jnp.where(which == 2, home[2] - 0.5, -1.0)))
        iso_part = total[3 * ROWS :]
        sums = []
        for c in range(3):
            both = scale * total[c * ROWS : (c + 1) * ROWS] + jnp.where(which == c, iso_part, 0.0)
            for shift in (64, 32, 16):
                both = both + pltpu.roll(both, shift, 1)
            sums += [both[8 * b : 8 * b + 8] for b in range(4)]
        first = sums[0]
        for g in range(1, 8):
            first = jnp.where(group == g, sums[g], first)
        second = sums[8]
        for g in range(1, 4):
            second = jnp.where(group % 4 == g, sums[8 + g], second)
        second = jnp.where(lane < 64, second, pltpu.roll(second, 4, 0))
        sent[step, 0:8] = first
        sent[step, 8:12] = second[0:4]

        @pl.when(offset != 0)
        def _():
            send(sent.at[step], landed.at[z], part_sem, device(x, y, tz, core))

        @pl.when(offset == 0)
        def _():
            landed[z] = sent[step]

        return carry

    lax.fori_loop(0, NZ, one_target, 0)

    wait(landed.at[pl.ds(0, NZ - 1)], part_sem)
    whole = landed[0]
    for k in range(1, NZ):
        whole = whole + landed[k]
    packed = jnp.concatenate([whole, jnp.zeros((LANES - 12, LANES), F32)], axis=0)
    turned = jnp.transpose(packed)
    out_lane = lax.broadcasted_iota(jnp.int32, (HALF, LANES), 1)
    for c in range(3):
        made = jnp.zeros((HALF, LANES), F32)
        for b in range(4):
            if c < 2:
                piece = turned[(c * 4 + b) * HALF : (c * 4 + b + 1) * HALF]
                made = jnp.where(out_lane // 8 == b, pltpu.roll(piece, 8 * b, 1) if b else piece, made)
            else:
                for u in range(2):
                    piece = turned[(u * 4 + b) * HALF : (u * 4 + b + 1) * HALF]
                    shift = (8 * b + 4 * u - 8) % LANES
                    made = jnp.where(out_lane // 4 == 2 * b + u, pltpu.roll(piece, shift, 1) if shift else piece, made)
        out_ref[c] = made[:, 0:ROWS]

    wait(target_row.at[pl.ds(0, 2 * REACH)], send_sem)
    wait(target_row.at[pl.ds(0, 2 * REACH - 1)], send_sem)
    wait(src_row.at[pl.ds(0, PLANE - 1)], send_sem)
    wait(src_block.at[pl.ds(0, PLANE - 1)], send_sem)
    wait(landed.at[pl.ds(0, NZ - 1)], send_sem)


def body(positions, forces):
    total = positions.shape[1] * lax.axis_size("blk") * lax.axis_size("quad")
    radius = radius_scale / total ** (1.0 / 3.0)
    dma = pltpu.SemaphoreType.DMA
    return pl.pallas_call(
        functools.partial(kernel, radius),
        out_shape=jax.ShapeDtypeStruct(forces.shape, F32),
        in_specs=[pl.BlockSpec(memory_space=pltpu.HBM)] * 2,
        out_specs=pl.BlockSpec(memory_space=pltpu.VMEM),
        scratch_shapes=[
            pltpu.VMEM((3, ROWS), F32),
            pltpu.VMEM((3, HALF, ROWS), F32),
            pltpu.VMEM((1, 1, LANES), F32),
            pltpu.VMEM((HALF, LANES), F32),
            pltpu.VMEM((PLANE, 1, LANES), F32),
            pltpu.VMEM((PLANE, HALF, LANES), F32),
            pltpu.VMEM((NZ, 1, LANES), F32),
            pltpu.VMEM((PLANE * ROWS, LANES), BF16),
            pltpu.VMEM((3, 8, PLANE * ROWS), F32),
            pltpu.VMEM((NZ, 12, LANES), F32),
            pltpu.VMEM((NZ, 12, LANES), F32),
            dma((2,)),
            dma,
            dma((3,)),
            dma,
            dma,
            dma,
            dma,
        ],
        compiler_params=pltpu.CompilerParams(collective_id=0, has_side_effects=True, vmem_limit_bytes=32 * 1024 * 1024),
    )(positions, forces)


def solution(mesh):
    in_specs = (P(None, ("blk", "quad")), P(None, None, ("blk", "quad")))
    out_specs = P(None, None, ("blk", "quad"))
    return jax.shard_map(body, mesh=mesh, in_specs=in_specs, out_specs=out_specs, check_vma=False)
```

time: 371 us -> 36.8 us (0.10)
  blocking collectives: 328 us -> 0 us
  Pallas kernels: 0 us -> 34.6 us
  matrix products: 17.5 us -> 0 us
  starting transfers between devices: 10.1 us -> 0 us
  other arithmetic: 6.63 us -> 0 us
  local copies, waits for them, and re-layouts: 7.87 us -> 2.03 us
    all_gather x1 -> x0, blocking collectives: 262 us -> none  [gather_turned(): whole = lax.all_gather(both, axis, axis=0, tiled=True)]
    all_to_all x1 -> x0, blocking collectives: 65.6 us -> none  [sent_and_summed(): tiles = lax.all_to_all(in_blocks(value, dim, peers), axis, 0, 0, tiled=True)]
    pallas_call x0 -> x1, Pallas kernels: none -> 34.6 us  [body(): pl.pallas_call(functools.partial(kernel, radius), out_shape=jax.ShapeDtyp...]
    dot_general x8 -> x0, matrix products: 17.5 us -> none  [one_block(): jnp.einsum('cdij,dvj->cvi', kernel, col_force, precision=lax.Precision.HI...]
    all_to_all x1 -> x0, starting transfers between devices: 10.1 us -> none  [copy_for_each(): lax.all_to_all(jnp.broadcast_to(value[None], (peers, *value.shape)), axis...]
  transfers between devices with their start and end apart: 1 -> 0, of which waited for: 0 -> 0; matrix products, arithmetic and copies ran while one was open for 2% -> 0% of each run, Pallas kernels for 0% -> 0%
where the time goes in v1:
time: 36.8 us; the launch traced here: 36.6 us
  Pallas kernels  34.6 us (94%)
  local copies, waits for them, and re-layouts  2.03 us (6%)
    pallas_call x1, Pallas kernels, body(): pl.pallas_call(functools.partial(kernel, radius), out_shape=jax.ShapeDtyp...  34.6 us
    unnamed x5, local copies, waits for them, and re-layouts  2.03 us

profile of v1, /device:TPU:1, one launch (start us, length us, event | category | flops | bytes accessed | tf_op | source)
XLA Modules:
  0.0 36.6 jit_solution(1239417319810071392)
XLA Ops:
  0.0 0.0 copy-start
  0.0 0.7 %copy-done = f32[3,16,32]{2,1,0:T(8,128)S(1)} copy-done((f32[3,16,32]{2,1,0:T(8,128)S(1)}, f32[3,16,32]{2,1,0:T(8,128)}, u32[]{:S(2)}) %copy-start) | copy-done | bytes 6168
  0.7 0.0 copy-start.1
  0.7 0.7 %copy-done.1 = f32[3,32]{1,0:T(4,128)S(1)} copy-done((f32[3,32]{1,0:T(4,128)S(1)}, f32[3,32]{1,0:T(4,128)}, u32[]{:S(2)}) %copy-start.1) | copy-done | bytes 408
  1.4 34.6 %shard_map.28 = f32[3,16,32]{2,1,0:T(8,128)S(1)} custom-call(f32[3,32]{1,0:T(4,128)S(1)} %copy-done.1, f32[3,16,32]{2,1,0:T(8,128)S(1)} %copy-done), custom_call_target="tpu_custom_call" | custom-call | tf_op jit(solution)/shard_map/pallas_call | solution.py:258
  36.0 0.6 %copy.4 = f32[3,16,32]{2,1,0:T(8,128)} copy(f32[3,16,32]{2,1,0:T(8,128)S(1)} %shard_map.28) | data formatting | bytes 12288
Async XLA Ops:
  0.0 0.7 %copy-start = (f32[3,16,32]{2,1,0:T(8,128)S(1)}, f32[3,16,32]{2,1,0:T(8,128)}, u32[]{:S(2)}) copy-start(f32[3,16,32]{2,1,0:T(8,128)} %force_hbm.1) | copy-start | bytes 18436
  0.7 0.7 %copy-start.1 = (f32[3,32]{1,0:T(4,128)S(1)}, f32[3,32]{1,0:T(4,128)}, u32[]{:S(2)}) copy-start(f32[3,32]{1,0:T(4,128)} %pos_hbm.1) | copy-start | bytes 1156

commit v2 on v1

--- a/solution.py
+++ b/solution.py
@@ -20,7 +20,6 @@
 ROWS = 32
 HALF = ROWS // 2
 GROUPS = LANES // HALF
-FILL = 4
 
 
 def place():
@@ -39,22 +38,12 @@
     return [o for o in far_first if o != (0, 0, 0)]
 
 
-def target_offset(step):
-    far = step - FILL
-    rest = step - (FILL + NZ - 1 - 2 * REACH)
-    sign = lambda odd: 1 - 2 * odd
-    first = (REACH - step // 2) * sign(step % 2)
-    middle = (NZ // 2 - (far + 1) // 2) * sign(1 - far % 2)
-    last = (REACH - FILL // 2 - rest // 2) * sign(rest % 2)
-    return jnp.where(step < FILL, first, jnp.where(far < NZ - 1 - 2 * REACH, middle, last))
-
-
 def widened(value):
     return jnp.concatenate([value, jnp.zeros((value.shape[0], LANES - ROWS), F32)], axis=1)
 
 
 def kernel(radius, pos_hbm, force_hbm, out_ref, pos_in, force_in, my_row, my_block, src_row, src_block, target_row,
-           weights, src_pos, sent, landed, in_sem, send_sem, near_sem, far_sem, row_sem, block_sem, part_sem):
+           weights, src_pos, sent, landed, in_sem, send_sem, line_sem, row_sem, block_sem, part_sem):
     x, y, z, core = place()
     plane_slot = x * GROUPS + y * 2 + core
     turn = (y * 2 + core) * HALF
@@ -102,8 +91,7 @@
         pltpu.make_async_remote_copy(src, dst, send_sem, sem, device_id=where, device_id_type=MESH).start()
 
     for k in line:
-        sem = near_sem.at[0 if k == -REACH else 1 if k == REACH else 2]
-        send(my_row.at[0], target_row.at[z], sem, on_line(k))
+        send(my_row.at[0], target_row.at[z], line_sem.at[z], on_line(k))
     for o in plane_peers():
         send(my_row.at[0], src_row.at[plane_slot], row_sem, in_plane(o))
     for o in plane_peers():
@@ -116,12 +104,12 @@
         pltpu.make_async_copy(ref, ref, sem).wait()
 
     up, down = (z + REACH) % NZ, (z + NZ - REACH) % NZ
-    wait(my_row.at[0], near_sem.at[0])
+    wait(target_row.at[up], line_sem.at[up])
     for k in range(REACH, 0, -1):
-        send(target_row.at[up], target_row.at[up], far_sem, on_line(-k))
-    wait(my_row.at[0], near_sem.at[1])
+        send(target_row.at[up], target_row.at[up], line_sem.at[up], on_line(-k))
+    wait(target_row.at[down], line_sem.at[down])
     for k in range(REACH - 1, 0, -1):
-        send(target_row.at[down], target_row.at[down], far_sem, on_line(k))
+        send(target_row.at[down], target_row.at[down], line_sem.at[down], on_line(k))
 
     wait(src_row.at[pl.ds(0, PLANE - 1)], row_sem)
     for tile in range(PLANE // GROUPS):
@@ -133,7 +121,6 @@
                 at = (h * PLANE // GROUPS + tile) * LANES
                 own = pltpu.roll(jnp.broadcast_to(own, (8, LANES)), (LANES - HALF * m) % LANES, 1)
                 src_pos[e, :, at : at + LANES] = own
-    wait(target_row.at[pl.ds(0, 2 * REACH - 2)], near_sem.at[2])
 
     wait(src_block.at[pl.ds(0, PLANE - 1)], block_sem)
     half_rows = PLANE * HALF
@@ -148,20 +135,22 @@
     near_sq = 4.0 * radius * radius
     lane_group = lax.broadcasted_iota(jnp.int32, (ROWS, LANES), 1) // HALF
 
-    def one_target(step, carry):
-        offset = target_offset(step)
-        tz = (z + offset + NZ) % NZ
-
-        @pl.when(step == FILL)
+    which = lane_group % 4
+
+    def arrived(tz):
+        @pl.when((tz < NZ) & (tz != z) & (tz != up) & (tz != down))
         def _():
-            wait(target_row.at[pl.ds(0, NZ - 1 - 2 * REACH)], far_sem)
-
+            wait(target_row.at[tz], line_sem.at[tz])
+
+    def columns(tz):
         theirs = pltpu.roll(jnp.broadcast_to(target_row[tz], (8, LANES)), LANES - turn, 1)
-        columns = jnp.transpose(jnp.broadcast_to(theirs[0:1], (LANES, LANES)))
-        home = [
-            jnp.concatenate([columns[e * HALF : (e + 1) * HALF], columns[(3 + e) * HALF : (4 + e) * HALF]], axis=0)
+        turned = jnp.transpose(jnp.broadcast_to(theirs[0:1], (LANES, LANES)))
+        return [
+            jnp.concatenate([turned[e * HALF : (e + 1) * HALF], turned[(3 + e) * HALF : (4 + e) * HALF]], axis=0)
             for e in range(3)
         ]
+
+    def pair_sums(home):
         total = jnp.zeros((4 * ROWS, LANES), F32)
         for p in range(2 * half_rows // wide):
             pieces = []
@@ -192,13 +181,17 @@
             tile = weights[p * wide : (p + 1) * wide, :]
             total += jnp.dot(upper, tile, preferred_element_type=F32)
             total += jnp.dot(lower, tile, preferred_element_type=F32)
-
-        which = lane_group % 4
-        scale = jnp.where(which == 0, home[0] - 0.5, jnp.where(which == 1, home[1] - 0.5, jnp.where(which == 2, home[2] - 0.5, -1.0)))
+        scale = jnp.where(
+            which == 0, home[0] - 0.5, jnp.where(which == 1, home[1] - 0.5, jnp.where(which == 2, home[2] - 0.5, -1.0))
+        )
         iso_part = total[3 * ROWS :]
+        return [
+            scale * total[c * ROWS : (c + 1) * ROWS] + jnp.where(which == c, iso_part, 0.0) for c in range(3)
+        ]
+
+    def fold(spread, tz):
         sums = []
-        for c in range(3):
-            both = scale * total[c * ROWS : (c + 1) * ROWS] + jnp.where(which == c, iso_part, 0.0)
+        for both in spread:
             for shift in (64, 32, 16):
                 both = both + pltpu.roll(both, shift, 1)
             sums += [both[8 * b : 8 * b + 8] for b in range(4)]
@@ -209,20 +202,32 @@
         for g in range(1, 4):
             second = jnp.where(group % 4 == g, sums[8 + g], second)
         second = jnp.where(lane < 64, second, pltpu.roll(second, 4, 0))
-        sent[step, 0:8] = first
-        sent[step, 8:12] = second[0:4]
-
-        @pl.when(offset != 0)
+        sent[tz, 0:8] = first
+        sent[tz, 8:12] = second[0:4]
+
+    def give(tz):
+        @pl.when((tz >= 0) & (tz != z))
         def _():
-            send(sent.at[step], landed.at[z], part_sem, device(x, y, tz, core))
-
-        @pl.when(offset == 0)
+            send(sent.at[tz], landed.at[z], part_sem, device(x, y, tz, core))
+
+        @pl.when(tz == z)
         def _():
-            landed[z] = sent[step]
-
-        return carry
-
-    lax.fori_loop(0, NZ, one_target, 0)
+            landed[z] = sent[z]
+
+    def one_target(tz, carry):
+        home, spread = carry
+        arrived(tz + 1)
+        later = columns(jnp.minimum(tz + 1, NZ - 1))
+        fold(spread, jnp.maximum(tz - 1, 0))
+        spread = pair_sums(home)
+        give(tz - 1)
+        return later, spread
+
+    arrived(0)
+    zeros = [jnp.zeros((ROWS, LANES), F32)] * 3
+    _, spread = lax.fori_loop(0, NZ, one_target, (columns(0), zeros))
+    fold(spread, NZ - 1)
+    give(jnp.int32(NZ - 1))
 
     wait(landed.at[pl.ds(0, NZ - 1)], part_sem)
     whole = landed[0]
@@ -274,14 +279,13 @@
             pltpu.VMEM((NZ, 12, LANES), F32),
             dma((2,)),
             dma,
-            dma((3,)),
-            dma,
+            dma((NZ,)),
             dma,
             dma,
             dma,
         ],
         compiler_params=pltpu.CompilerParams(collective_id=0, has_side_effects=True, vmem_limit_bytes=32 * 1024 * 1024),
-    )(positions, forces)
+    )(*(pltpu.with_memory_space_constraint(a, pltpu.HBM) for a in (positions, forces)))
 
 
 def solution(mesh):

time: 36.8 us -> 31.5 us (0.86)
  the two profiles are of different devices: /device:TPU:1 before, /device:TPU:32 now
where the time goes in v2:
time: 31.5 us; the launch traced here: 31.3 us
  Pallas kernels  30.7 us (97%)
  local copies, waits for them, and re-layouts  0.61 us (2%)
    pallas_call x1, Pallas kernels, body(): pl.pallas_call(functools.partial(kernel, radius), out_shape=jax.ShapeDtyp...  30.7 us

profile of v2, /device:TPU:32, one launch (start us, length us, event | category | flops | bytes accessed | tf_op | source)
XLA Modules:
  0.0 31.3 jit_solution(4315124676945430562)
XLA Ops:
  0.0 30.7 %shard_map.28 = f32[3,16,32]{2,1,0:T(8,128)S(1)} custom-call(f32[3,32]{1,0:T(4,128)} %pos_hbm.1, f32[3,16,32]{2,1,0:T(8,128)} %force_hbm.1), custom_call_target="tpu_custom_call" | custom-call | tf_op jit(solution)/shard_map/pallas_call | solution.py:263
  30.7 0.6 %copy.4 = f32[3,16,32]{2,1,0:T(8,128)} copy(f32[3,16,32]{2,1,0:T(8,128)S(1)} %shard_map.28) | data formatting | bytes 12288

commit v3 on v2

--- a/solution.py
+++ b/solution.py
@@ -14,12 +14,14 @@
 radius_scale = 0.3
 
 NX, NY, NZ = 4, 4, 16
-PLANE = NX * NY * 2
+CHIPS = NX * NY
+PLANE = CHIPS * 2
 REACH = NZ // 4
 LANES = 128
 ROWS = 32
 HALF = ROWS // 2
 GROUPS = LANES // HALF
+SOON = 12
 
 
 def place():
@@ -32,10 +34,12 @@
     return ((y * 2 + x % 2) * NZ + z, (x // 2) * 2 + core)
 
 
-def plane_peers():
-    offsets = [(a, b, c) for a in range(NX) for b in range(NY) for c in range(2)]
-    far_first = sorted(offsets, key=lambda o: -(min(o[0], NX - o[0]) + min(o[1], NY - o[1])))
-    return [o for o in far_first if o != (0, 0, 0)]
+def slot_of(x, y):
+    return (x // 2) * 8 + (y // 2) * 4 + (x % 2) * 2 + y % 2
+
+
+def slot_device(slot, z, core):
+    return device((slot // 8) * 2 + (slot // 2) % 2, ((slot // 4) % 2) * 2 + slot % 2, z, core)
 
 
 def widened(value):
@@ -43,18 +47,16 @@
 
 
 def kernel(radius, pos_hbm, force_hbm, out_ref, pos_in, force_in, my_row, my_block, src_row, src_block, target_row,
-           weights, src_pos, sent, landed, in_sem, send_sem, line_sem, row_sem, block_sem, part_sem):
+           weights, src_pos, sent, landed, in_sem, send_sem, line_sem, row_sem, block_sem, part_sem, open_sem):
     x, y, z, core = place()
-    plane_slot = x * GROUPS + y * 2 + core
-    turn = (y * 2 + core) * HALF
+    plane_slot = slot_of(x, y)
+    sibling = device(x, y, z, 1 - core)
+    turn = (plane_slot % GROUPS) * HALF
     load_pos = pltpu.make_async_copy(pos_hbm, pos_in, in_sem.at[0])
     load_force = pltpu.make_async_copy(force_hbm, force_in, in_sem.at[1])
     load_pos.start()
     load_force.start()
 
-    def in_plane(o):
-        return device((x + o[0]) % NX, (y + o[1]) % NY, z, (core + o[2]) % 2)
-
     def on_line(k):
         return device(x, y, (z + k + NZ) % NZ, core)
 
@@ -62,8 +64,11 @@
     barrier = pltpu.get_barrier_semaphore()
     for k in line:
         pl.semaphore_signal(barrier, 1, device_id=on_line(k), device_id_type=MESH)
-    for o in plane_peers():
-        pl.semaphore_signal(barrier, 1, device_id=in_plane(o), device_id_type=MESH)
+    @pl.loop(0, CHIPS - 1 - plane_slot)
+    def _(k):
+        pl.semaphore_signal(barrier, 1, device_id=slot_device(CHIPS - 1 - k, z, core), device_id_type=MESH)
+
+    pl.semaphore_signal(barrier, 1, device_id=sibling, device_id_type=MESH)
 
     lane = lax.broadcasted_iota(jnp.int32, (8, LANES), 1)
     sub = lax.broadcasted_iota(jnp.int32, (8, LANES), 0)
@@ -85,23 +90,36 @@
     stack = jnp.concatenate([stack, pltpu.roll(stack, LANES - HALF, 1)], axis=0)
     my_block[...] = jnp.transpose(stack)[0:HALF]
 
-    pl.semaphore_wait(barrier, len(line) + len(plane_peers()))
+    pl.semaphore_wait(barrier, len(line) + 1 + plane_slot)
 
     def send(src, dst, sem, where):
         pltpu.make_async_remote_copy(src, dst, send_sem, sem, device_id=where, device_id_type=MESH).start()
 
     for k in line:
         send(my_row.at[0], target_row.at[z], line_sem.at[z], on_line(k))
-    for o in plane_peers():
-        send(my_row.at[0], src_row.at[plane_slot], row_sem, in_plane(o))
-    for o in plane_peers():
-        send(my_block, src_block.at[plane_slot], block_sem, in_plane(o))
-    src_row[plane_slot] = my_row[0]
-    src_block[plane_slot] = my_block[...]
+    def send_sources(slot):
+        send(my_row.at[0], src_row.at[0, plane_slot], row_sem.at[0], slot_device(slot, z, core))
+        send(my_block, src_block.at[0, plane_slot], block_sem.at[0], slot_device(slot, z, core))
+
+    @pl.loop(0, plane_slot)
+    def _(slot):
+        pl.semaphore_signal(open_sem.at[plane_slot], 1, device_id=slot_device(slot, z, core), device_id_type=MESH)
+        send_sources(slot)
+
+    src_row[0, plane_slot] = my_row[0]
+    src_block[0, plane_slot] = my_block[...]
     target_row[z] = my_row[0]
 
     def wait(ref, sem):
         pltpu.make_async_copy(ref, ref, sem).wait()
+
+    def open_to(first, last):
+        @pl.loop(first, last)
+        def _(slot):
+            pl.semaphore_wait(open_sem.at[slot], 1)
+            send_sources(slot)
+
+    open_to(plane_slot + 1, jnp.maximum(plane_slot + 1, SOON))
 
     up, down = (z + REACH) % NZ, (z + NZ - REACH) % NZ
     wait(target_row.at[up], line_sem.at[up])
@@ -111,25 +129,40 @@
     for k in range(REACH - 1, 0, -1):
         send(target_row.at[down], target_row.at[down], line_sem.at[down], on_line(k))
 
-    wait(src_row.at[pl.ds(0, PLANE - 1)], row_sem)
-    for tile in range(PLANE // GROUPS):
-        rows = jnp.concatenate([src_row[tile * GROUPS + k] for k in range(GROUPS)], axis=0)
-        for h in range(2):
-            for e in range(3):
-                m = 3 * h + e
-                own = jnp.sum(jnp.where((group - sub - m + 2 * GROUPS) % GROUPS == 0, rows, 0.0), axis=0, keepdims=True)
-                at = (h * PLANE // GROUPS + tile) * LANES
-                own = pltpu.roll(jnp.broadcast_to(own, (8, LANES)), (LANES - HALF * m) % LANES, 1)
-                src_pos[e, :, at : at + LANES] = own
-
-    wait(src_block.at[pl.ds(0, PLANE - 1)], block_sem)
+    open_to(jnp.maximum(plane_slot + 1, SOON), CHIPS)
+
     half_rows = PLANE * HALF
-    value = src_block[...].reshape(half_rows, LANES)
-    high = value.astype(BF16).astype(F32)
-    low = value - high
-    left = lax.broadcasted_iota(jnp.int32, (half_rows, LANES), 1) < LANES // 2
-    weights[0:half_rows] = jnp.where(left, high, pltpu.roll(low, LANES // 2, 1)).astype(BF16)
-    weights[half_rows:] = jnp.where(left, pltpu.roll(high, LANES // 2, 1), low).astype(BF16)
+    core_rows = CHIPS * HALF
+    left = lax.broadcasted_iota(jnp.int32, (core_rows, LANES), 1) < LANES // 2
+
+    def prepare(i):
+        for tile in range(CHIPS // GROUPS):
+            rows = jnp.concatenate([src_row[i, tile * GROUPS + k] for k in range(GROUPS)], axis=0)
+            for h in range(2):
+                for e in range(3):
+                    m = 3 * h + e
+                    own = jnp.sum(
+                        jnp.where((group - sub - m + 2 * GROUPS) % GROUPS == 0, rows, 0.0), axis=0, keepdims=True
+                    )
+                    at = (h * (PLANE // GROUPS) + i * (CHIPS // GROUPS) + tile) * LANES
+                    own = pltpu.roll(jnp.broadcast_to(own, (8, LANES)), (LANES - HALF * m) % LANES, 1)
+                    src_pos[e, :, at : at + LANES] = own
+        value = src_block[i].reshape(core_rows, LANES)
+        high = value.astype(BF16).astype(F32)
+        low = value - high
+        at = i * core_rows
+        weights[at : at + core_rows] = jnp.where(left, high, pltpu.roll(low, LANES // 2, 1)).astype(BF16)
+        at = at + half_rows
+        weights[at : at + core_rows] = jnp.where(left, pltpu.roll(high, LANES // 2, 1), low).astype(BF16)
+
+    wait(src_row.at[0, pl.ds(0, CHIPS - 1)], row_sem.at[0])
+    send(src_row.at[0], src_row.at[1], row_sem.at[1], sibling)
+    wait(src_block.at[0, pl.ds(0, CHIPS - 1)], block_sem.at[0])
+    send(src_block.at[0], src_block.at[1], block_sem.at[1], sibling)
+    prepare(0)
+    wait(src_row.at[1], row_sem.at[1])
+    wait(src_block.at[1], block_sem.at[1])
+    prepare(1)
 
     wide = 2 * LANES
     near_sq = 4.0 * radius * radius
@@ -179,8 +212,9 @@
             upper = exact.astype(BF16)
             lower = (exact - upper.astype(F32)).astype(BF16)
             tile = weights[p * wide : (p + 1) * wide, :]
-            total += jnp.dot(upper, tile, preferred_element_type=F32)
-            total += jnp.dot(lower, tile, preferred_element_type=F32)
+            total += jnp.dot(
+                jnp.concatenate([upper, lower], axis=1), jnp.concatenate([tile, tile], axis=0), preferred_element_type=F32
+            )
         scale = jnp.where(
             which == 0, home[0] - 0.5, jnp.where(which == 1, home[1] - 0.5, jnp.where(which == 2, home[2] - 0.5, -1.0))
         )
@@ -251,8 +285,10 @@
 
     wait(target_row.at[pl.ds(0, 2 * REACH)], send_sem)
     wait(target_row.at[pl.ds(0, 2 * REACH - 1)], send_sem)
-    wait(src_row.at[pl.ds(0, PLANE - 1)], send_sem)
-    wait(src_block.at[pl.ds(0, PLANE - 1)], send_sem)
+    wait(src_row.at[0, pl.ds(0, CHIPS - 1)], send_sem)
+    wait(src_row.at[1], send_sem)
+    wait(src_block.at[0, pl.ds(0, CHIPS - 1)], send_sem)
+    wait(src_block.at[1], send_sem)
     wait(landed.at[pl.ds(0, NZ - 1)], send_sem)
 
 
@@ -270,8 +306,8 @@
             pltpu.VMEM((3, HALF, ROWS), F32),
             pltpu.VMEM((1, 1, LANES), F32),
             pltpu.VMEM((HALF, LANES), F32),
-            pltpu.VMEM((PLANE, 1, LANES), F32),
-            pltpu.VMEM((PLANE, HALF, LANES), F32),
+            pltpu.VMEM((2, CHIPS, 1, LANES), F32),
+            pltpu.VMEM((2, CHIPS, HALF, LANES), F32),
             pltpu.VMEM((NZ, 1, LANES), F32),
             pltpu.VMEM((PLANE * ROWS, LANES), BF16),
             pltpu.VMEM((3, 8, PLANE * ROWS), F32),
@@ -280,9 +316,10 @@
             dma((2,)),
             dma,
             dma((NZ,)),
+            dma((2,)),
+            dma((2,)),
             dma,
-            dma,
-            dma,
+            pltpu.SemaphoreType.REGULAR((CHIPS,)),
         ],
         compiler_params=pltpu.CompilerParams(collective_id=0, has_side_effects=True, vmem_limit_bytes=32 * 1024 * 1024),
     )(*(pltpu.with_memory_space_constraint(a, pltpu.HBM) for a in (positions, forces)))

time: 31.5 us -> 31.3 us (level)
  the two profiles are of different devices: /device:TPU:32 before, /device:TPU:6 now
where the time goes in v3:
time: 31.3 us; the launch traced here: 30.9 us
  Pallas kernels  30.3 us (97%)
  local copies, waits for them, and re-layouts  0.61 us (2%)
    pallas_call x1, Pallas kernels, body(): pl.pallas_call(functools.partial(kernel, radius), out_shape=jax.ShapeDtyp...  30.3 us

profile of v3, /device:TPU:6, one launch (start us, length us, event | category | flops | bytes accessed | tf_op | source)
XLA Modules:
  0.0 30.9 jit_solution(10124922916122883528)
XLA Ops:
  0.0 30.3 %shard_map.28 = f32[3,16,32]{2,1,0:T(8,128)S(1)} custom-call(f32[3,32]{1,0:T(4,128)} %pos_hbm.1, f32[3,16,32]{2,1,0:T(8,128)} %force_hbm.1), custom_call_target="tpu_custom_call" | custom-call | tf_op jit(solution)/shard_map/pallas_call | solution.py:299
  30.3 0.6 %copy.4 = f32[3,16,32]{2,1,0:T(8,128)} copy(f32[3,16,32]{2,1,0:T(8,128)S(1)} %shard_map.28) | data formatting | bytes 12288

commit v4 on v3

--- a/solution.py
+++ b/solution.py
@@ -51,6 +51,8 @@
     x, y, z, core = place()
     plane_slot = slot_of(x, y)
     sibling = device(x, y, z, 1 - core)
+    early = plane_slot < SOON
+    met = jnp.where(early, SOON, CHIPS)
     turn = (plane_slot % GROUPS) * HALF
     load_pos = pltpu.make_async_copy(pos_hbm, pos_in, in_sem.at[0])
     load_force = pltpu.make_async_copy(force_hbm, force_in, in_sem.at[1])
@@ -64,9 +66,11 @@
     barrier = pltpu.get_barrier_semaphore()
     for k in line:
         pl.semaphore_signal(barrier, 1, device_id=on_line(k), device_id_type=MESH)
-    @pl.loop(0, CHIPS - 1 - plane_slot)
-    def _(k):
-        pl.semaphore_signal(barrier, 1, device_id=slot_device(CHIPS - 1 - k, z, core), device_id_type=MESH)
+    @pl.loop(jnp.where(early, 0, SOON), CHIPS)
+    def _(slot):
+        @pl.when(slot != plane_slot)
+        def _():
+            pl.semaphore_signal(barrier, 1, device_id=slot_device(slot, z, core), device_id_type=MESH)
 
     pl.semaphore_signal(barrier, 1, device_id=sibling, device_id_type=MESH)
 
@@ -90,7 +94,7 @@
     stack = jnp.concatenate([stack, pltpu.roll(stack, LANES - HALF, 1)], axis=0)
     my_block[...] = jnp.transpose(stack)[0:HALF]
 
-    pl.semaphore_wait(barrier, len(line) + 1 + plane_slot)
+    pl.semaphore_wait(barrier, len(line) + met)
 
     def send(src, dst, sem, where):
         pltpu.make_async_remote_copy(src, dst, send_sem, sem, device_id=where, device_id_type=MESH).start()
@@ -101,10 +105,15 @@
         send(my_row.at[0], src_row.at[0, plane_slot], row_sem.at[0], slot_device(slot, z, core))
         send(my_block, src_block.at[0, plane_slot], block_sem.at[0], slot_device(slot, z, core))
 
-    @pl.loop(0, plane_slot)
+    @pl.loop(0, met)
     def _(slot):
-        pl.semaphore_signal(open_sem.at[plane_slot], 1, device_id=slot_device(slot, z, core), device_id_type=MESH)
-        send_sources(slot)
+        @pl.when(jnp.logical_not(early) & (slot < SOON))
+        def _():
+            pl.semaphore_signal(open_sem.at[plane_slot], 1, device_id=slot_device(slot, z, core), device_id_type=MESH)
+
+        @pl.when(slot != plane_slot)
+        def _():
+            send_sources(slot)
 
     src_row[0, plane_slot] = my_row[0]
     src_block[0, plane_slot] = my_block[...]
@@ -112,14 +121,6 @@
 
     def wait(ref, sem):
         pltpu.make_async_copy(ref, ref, sem).wait()
-
-    def open_to(first, last):
-        @pl.loop(first, last)
-        def _(slot):
-            pl.semaphore_wait(open_sem.at[slot], 1)
-            send_sources(slot)
-
-    open_to(plane_slot + 1, jnp.maximum(plane_slot + 1, SOON))
 
     up, down = (z + REACH) % NZ, (z + NZ - REACH) % NZ
     wait(target_row.at[up], line_sem.at[up])
@@ -129,7 +130,10 @@
     for k in range(REACH - 1, 0, -1):
         send(target_row.at[down], target_row.at[down], line_sem.at[down], on_line(k))
 
-    open_to(jnp.maximum(plane_slot + 1, SOON), CHIPS)
+    @pl.loop(met, CHIPS)
+    def _(slot):
+        pl.semaphore_wait(open_sem.at[slot], 1)
+        send_sources(slot)
 
     half_rows = PLANE * HALF
     core_rows = CHIPS * HALF

time: 31.3 us -> 31.2 us (level)
  no operation moved by 1% of the time
where the time goes in v4:
time: 31.2 us; the launch traced here: 31.1 us
  Pallas kernels  30.4 us (97%)
  local copies, waits for them, and re-layouts  0.61 us (2%)
    pallas_call x1, Pallas kernels, body(): pl.pallas_call(functools.partial(kernel, radius), out_shape=jax.ShapeDtyp...  30.4 us

profile of v4, /device:TPU:6, one launch (start us, length us, event | category | flops | bytes accessed | tf_op | source)
XLA Modules:
  0.0 31.1 jit_solution(9711376096984852374)
XLA Ops:
  0.0 30.4 %shard_map.28 = f32[3,16,32]{2,1,0:T(8,128)S(1)} custom-call(f32[3,32]{1,0:T(4,128)} %pos_hbm.1, f32[3,16,32]{2,1,0:T(8,128)} %force_hbm.1), custom_call_target="tpu_custom_call" | custom-call | tf_op jit(solution)/shard_map/pallas_call | solution.py:303
  30.4 0.6 %copy.4 = f32[3,16,32]{2,1,0:T(8,128)} copy(f32[3,16,32]{2,1,0:T(8,128)S(1)} %shard_map.28) | data formatting | bytes 12288

commit v5 on v4

--- a/solution.py
+++ b/solution.py
@@ -123,17 +123,17 @@
         pltpu.make_async_copy(ref, ref, sem).wait()
 
     up, down = (z + REACH) % NZ, (z + NZ - REACH) % NZ
+    @pl.loop(met, CHIPS)
+    def _(slot):
+        pl.semaphore_wait(open_sem.at[slot], 1)
+        send_sources(slot)
+
     wait(target_row.at[up], line_sem.at[up])
     for k in range(REACH, 0, -1):
         send(target_row.at[up], target_row.at[up], line_sem.at[up], on_line(-k))
     wait(target_row.at[down], line_sem.at[down])
     for k in range(REACH - 1, 0, -1):
         send(target_row.at[down], target_row.at[down], line_sem.at[down], on_line(k))
-
-    @pl.loop(met, CHIPS)
-    def _(slot):
-        pl.semaphore_wait(open_sem.at[slot], 1)
-        send_sources(slot)
 
     half_rows = PLANE * HALF
     core_rows = CHIPS * HALF

time: 31.2 us -> 31.2 us (level)
  no operation moved by 1% of the time
where the time goes in v5:
time: 31.2 us; the launch traced here: 31.1 us
  Pallas kernels  30.4 us (97%)
  local copies, waits for them, and re-layouts  0.61 us (2%)
    pallas_call x1, Pallas kernels, body(): pl.pallas_call(functools.partial(kernel, radius), out_shape=jax.ShapeDtyp...  30.4 us

profile of v5, /device:TPU:6, one launch (start us, length us, event | category | flops | bytes accessed | tf_op | source)
XLA Modules:
  0.0 31.1 jit_solution(9151292810412090486)
XLA Ops:
  0.0 30.4 %shard_map.28 = f32[3,16,32]{2,1,0:T(8,128)S(1)} custom-call(f32[3,32]{1,0:T(4,128)} %pos_hbm.1, f32[3,16,32]{2,1,0:T(8,128)} %force_hbm.1), custom_call_target="tpu_custom_call" | custom-call | tf_op jit(solution)/shard_map/pallas_call | solution.py:303
  30.4 0.6 %copy.4 = f32[3,16,32]{2,1,0:T(8,128)} copy(f32[3,16,32]{2,1,0:T(8,128)S(1)} %shard_map.28) | data formatting | bytes 12288

commit v6 on v4

--- a/solution.py
+++ b/solution.py
@@ -181,7 +181,7 @@
 
     def columns(tz):
         theirs = pltpu.roll(jnp.broadcast_to(target_row[tz], (8, LANES)), LANES - turn, 1)
-        turned = jnp.transpose(jnp.broadcast_to(theirs[0:1], (LANES, LANES)))
+        turned = jnp.broadcast_to(jnp.transpose(theirs)[:, 0:1], (LANES, LANES))
         return [
             jnp.concatenate([turned[e * HALF : (e + 1) * HALF], turned[(3 + e) * HALF : (4 + e) * HALF]], axis=0)
             for e in range(3)

time: 31.2 us -> 31.2 us (level)
  no operation moved by 1% of the time
where the time goes in v6:
time: 31.2 us; the launch traced here: 31.1 us
  Pallas kernels  30.5 us (98%)
  local copies, waits for them, and re-layouts  0.61 us (2%)
    pallas_call x1, Pallas kernels, body(): pl.pallas_call(functools.partial(kernel, radius), out_shape=jax.ShapeDtyp...  30.5 us

profile of v6, /device:TPU:6, one launch (start us, length us, event | category | flops | bytes accessed | tf_op | source)
XLA Modules:
  0.0 31.1 jit_solution(15179229737700985717)
XLA Ops:
  0.0 30.5 %shard_map.28 = f32[3,16,32]{2,1,0:T(8,128)S(1)} custom-call(f32[3,32]{1,0:T(4,128)} %pos_hbm.1, f32[3,16,32]{2,1,0:T(8,128)} %force_hbm.1), custom_call_target="tpu_custom_call" | custom-call | tf_op jit(solution)/shard_map/pallas_call | solution.py:303
  30.5 0.6 %copy.4 = f32[3,16,32]{2,1,0:T(8,128)} copy(f32[3,16,32]{2,1,0:T(8,128)S(1)} %shard_map.28) | data formatting | bytes 12288

commit v7 on v5

--- a/solution.py
+++ b/solution.py
@@ -181,7 +181,7 @@
 
     def columns(tz):
         theirs = pltpu.roll(jnp.broadcast_to(target_row[tz], (8, LANES)), LANES - turn, 1)
-        turned = jnp.transpose(jnp.broadcast_to(theirs[0:1], (LANES, LANES)))
+        turned = jnp.broadcast_to(jnp.transpose(theirs)[:, 0:1], (LANES, LANES))
         return [
             jnp.concatenate([turned[e * HALF : (e + 1) * HALF], turned[(3 + e) * HALF : (4 + e) * HALF]], axis=0)
             for e in range(3)

time: 31.2 us -> 31.2 us (level)
  no operation moved by 1% of the time
where the time goes in v7:
time: 31.2 us; the launch traced here: 31.1 us
  Pallas kernels  30.5 us (98%)
  local copies, waits for them, and re-layouts  0.61 us (2%)
    pallas_call x1, Pallas kernels, body(): pl.pallas_call(functools.partial(kernel, radius), out_shape=jax.ShapeDtyp...  30.5 us

profile of v7, /device:TPU:6, one launch (start us, length us, event | category | flops | bytes accessed | tf_op | source)
XLA Modules:
  0.0 31.1 jit_solution(6565801653842847754)
XLA Ops:
  0.0 30.5 %shard_map.28 = f32[3,16,32]{2,1,0:T(8,128)S(1)} custom-call(f32[3,32]{1,0:T(4,128)} %pos_hbm.1, f32[3,16,32]{2,1,0:T(8,128)} %force_hbm.1), custom_call_target="tpu_custom_call" | custom-call | tf_op jit(solution)/shard_map/pallas_call | solution.py:303
  30.5 0.6 %copy.4 = f32[3,16,32]{2,1,0:T(8,128)} copy(f32[3,16,32]{2,1,0:T(8,128)S(1)} %shard_map.28) | data formatting | bytes 12288
